TPU v7x, 32 devices: a whole 2x2x4 slice. The times are simulated.
32 devices in a mesh: exp: 16 (over z, y, core), hid: 2 (over x).
Axes of the slice: x: 2, y: 2, z: 4, core: 2. Of those that a mesh axis runs over, the one named last changes fastest.
Arguments:
- tokens: bfloat16 [128, 2048], P(('exp', 'hid')), may hold values from -6 to 6
- grad_out: bfloat16 [128, 2048], P(('exp', 'hid')), may hold values from -3 to 3
- router_logits: float32 [128, 16], P(('exp', 'hid')), may hold values from -12 to 330
- selected: int32 [128, 8], P(('exp', 'hid')), may hold values from 0 to 15, as said below
- router_w: bfloat16 [2048, 16], replicated, may hold values from -0.59765625 to 0.59765625
- w_gate: bfloat16 [32, 2048, 384], P(('exp', 'hid')), may hold values from -0.125 to 0.125
- w_up: bfloat16 [32, 2048, 384], P(('exp', 'hid')), may hold values from -0.125 to 0.125
- w_down: bfloat16 [32, 384, 2048], P(('exp', 'hid')), may hold values from -0.21875 to 0.21875
Outputs:
- x_grad: bfloat16 [128, 2048], P(('exp', 'hid'))
- router_grad: float32 [2048, 16], P(('exp', 'hid'))
Inputs may be any that keep to these rules, and one draw needn't show every extreme that they name: `selected`: each row names 8 different experts; within each aligned block of 8 rows (the tokens of one index of exp) no expert is named by more than 8 rows, and in every block some expert is named by exactly 8 rows.
All inputs are finite; a program needn't handle non-finite values.
Results may differ from a plain program's by a relative error of at most 0.0075.
Values may be sent and summed in bfloat16 or wider, within the bound.
No kernel may reach another device: no remote copies, remote signals or barrier semaphores. Data moves between devices by JAX's collectives and lax.ppermute only.
A program may use at most 64 MiB of HBM per device.

v0:
```python
import functools

import jax
import jax.numpy as jnp
from jax import lax
from jax.experimental import pallas as pl
from jax.experimental.pallas import tpu as pltpu
from jax.sharding import PartitionSpec as P

AXES = ("exp", "hid")
LANES = 128
PIECES = 4
SCORE_PIECES = 2
VMEM_SPEC = pl.BlockSpec(memory_space=pltpu.VMEM)
HBM_SPEC = pl.BlockSpec(memory_space=pltpu.HBM)
F32 = jnp.float32
BF16 = jnp.bfloat16
NT = (((1,), (1,)), ((), ()))
TN = (((0,), (0,)), ((), ()))
PARAMS = pltpu.CompilerParams(vmem_limit_bytes=24 * 2**20)


def stage_masks(exp_size, hid_size):
    hid_bits = hid_size.bit_length() - 1
    all_bits = (exp_size * hid_size).bit_length() - 1
    core = hid_bits
    first = list(range(max(core + 1, all_bits - 2), all_bits))
    middle = [b for b in range(all_bits) if b != core and b not in first]
    groups = [first] + [middle[i : i + 2] for i in range(0, len(middle), 2)]
    bases = [[sum(1 << b for b in group[i:]) for i in range(len(group))] for group in groups]
    return bases, 1 << core


def group_masks(basis):
    masks = [0]
    for mask in basis:
        masks = masks + [m ^ mask for m in masks]
    return masks


def near_first(basis):
    return [a ^ b for a, b in zip(basis, basis[1:] + [0])]


def swap(block, mask, count):
    return lax.ppermute(block, AXES, [(i, i ^ mask) for i in range(count)])


def swaps(block, masks, count):
    return [swap(block, m, count) for m in masks]


def forward(blocks):
    return blocks[:1] + blocks[:0:-1]


def place_mask(place, basis):
    total = jnp.zeros_like(place)
    for digit, mask in enumerate(basis):
        total = total ^ (((place >> digit) & 1) * mask)
    return total


def own_index():
    return lax.axis_index("exp") * lax.axis_size("hid") + lax.axis_index("hid")


def in_hbm(*arrays):
    return tuple(pltpu.with_memory_space_constraint(a, pltpu.HBM) for a in arrays)


def softmax_f32(values):
    raised = jnp.exp(values - jnp.max(values, axis=-1, keepdims=True))
    return raised / jnp.sum(raised, axis=-1, keepdims=True)


def prep_kernel(tokens_in, grad_in, logits_in, chosen_in, out_ref, logits_ref, chosen_ref, sems):
    tok, width = tokens_in.shape
    pairs = [
        (logits_in, logits_ref),
        (chosen_in, chosen_ref),
        (tokens_in, out_ref.at[0, :, 0:width]),
        (grad_in, out_ref.at[1, :, 0:width]),
    ]
    copies = [pltpu.make_async_copy(src, dst, sems.at[i]) for i, (src, dst) in enumerate(pairs)]
    for copy in copies:
        copy.start()
    copies[0].wait()
    copies[1].wait()
    logits = logits_ref[...]
    chosen = chosen_ref[...]
    experts = logits.shape[1]
    ids = lax.broadcasted_iota(jnp.int32, logits.shape, 1)
    hit = ids == chosen[:, 0:1]
    for k in range(1, chosen.shape[1]):
        hit = hit | (ids == chosen[:, k : k + 1])
    top = jnp.max(jnp.where(hit, logits, -jnp.inf), axis=1, keepdims=True)
    raised = jnp.where(hit, jnp.exp(jnp.minimum(logits - top, 0.0)), 0.0)
    parts = [raised / jnp.sum(raised, axis=1, keepdims=True)]
    rest = softmax_f32(logits)
    for _ in range(PIECES - 1):
        parts.append(rest)
        rest = rest - rest.astype(BF16).astype(F32)
    lanes = out_ref.shape[2] - width
    spare = lanes - PIECES * experts
    extras = jnp.concatenate(parts + ([jnp.zeros((tok, spare), F32)] if spare else []), axis=1)
    out_ref[0, :, width:] = extras.astype(BF16)
    out_ref[1, :, width:] = jnp.zeros((tok, lanes), BF16)
    copies[2].wait()
    copies[3].wait()


def load_kernel(chunks, block_in, gate_in, up_in, down_in, block_ref, pair_ref, down_ref, sems):
    copies = []

    def add(src, dst):
        copies.append(pltpu.make_async_copy(src, dst, sems.at[len(copies)]))

    hidden, width = down_ref.shape
    for c in range(chunks):
        part = pl.ds(c * (width // chunks), width // chunks)
        add(gate_in.at[0, part, :], pair_ref.at[part, 0:hidden])
        add(up_in.at[0, part, :], pair_ref.at[part, hidden : 2 * hidden])
        part = pl.ds(c * (hidden // chunks), hidden // chunks)
        add(down_in.at[0, part, :], down_ref.at[part, :])
    add(block_in, block_ref)
    for copy in copies:
        copy.start()
    for copy in copies:
        copy.wait()


def join_kernel(*refs):
    blocks, out_ref, rows_ref = forward(refs[:-2]), refs[-2], refs[-1]
    count = len(blocks)
    tok = blocks[0].shape[1]
    for kind in range(2):
        for j, ref in enumerate(blocks):
            first = (kind * count + j) * tok
            rows_ref[first : first + tok, :] = ref[kind].astype(F32)
    out_ref[...] = rows_ref[...].astype(BF16)


def stack_kernel(*refs):
    out_ref = refs[-1]
    rows = refs[0].shape[0]
    for j, ref in enumerate(refs[:-1]):
        out_ref[j * rows : (j + 1) * rows, :] = ref[...]


def token_rows(refs, start, rows, group, kind, columns):
    parts = []
    for ref in refs:
        for j in range(rows // (2 * group)):
            first = start + (2 * j + kind) * group
            if not isinstance(first, int):
                first = pl.multiple_of(first, group)
            parts.append(ref[pl.ds(first, group), columns])
    return parts[0] if len(parts) == 1 else jnp.concatenate(parts, axis=0)


def put_scores(out_ref, scores_ref, width):
    rows = out_ref.shape[0]
    for c in range((out_ref.shape[1] - width) // LANES):
        out_ref[:, width + c * LANES : width + (c + 1) * LANES] = scores_ref[c * rows : (c + 1) * rows, :].astype(BF16)


def get_scores(in_ref, scores_ref, base, size, width):
    rows = in_ref.shape[0]
    for c in range(-(-size // rows)):
        here = min(rows, size - c * rows)
        tall = min(rows, -(-here // 16) * 16)
        block = in_ref[0:tall, width + c * LANES : width + (c + 1) * LANES].astype(F32)
        scores_ref[base + c * rows : base + c * rows + here, :] = block[:here]


def units_kernel(basis, group, tok, core_mask, blocks, *refs):
    own_refs, other_refs = forward(refs[:blocks]), forward(refs[blocks : 2 * blocks])
    pair_ref, down_ref, kept_ref, message_ref, pieces_ref, score_ref, padded_ref = refs[2 * blocks :]
    hidden, width = down_ref.shape
    rows, buf_width = own_refs[0].shape
    tokens = score_ref.shape[1]
    own = own_index()

    def terms(sets, start, step):
        act = token_rows(sets, start, step, group, 0, slice(None))
        count = act.shape[0]
        extras = act[:, width:].astype(F32)
        lane = lax.broadcasted_iota(jnp.int32, (count, buf_width - width), 1)
        column = jnp.sum(jnp.where(lane == own // 2, extras, 0.0), axis=1, keepdims=True)
        pair = jnp.dot(act[:, :width], pair_ref[...], preferred_element_type=F32)
        gate_pre = pair[:, :hidden]
        up_pre = pair[:, hidden:]
        cot = token_rows(sets, start, step, group, 1, slice(0, width))
        back = lax.dot_general(cot, down_ref[...], NT, preferred_element_type=F32)
        sig = jax.nn.sigmoid(gate_pre)
        act_gate = gate_pre * sig
        score = jnp.sum(act_gate * up_pre * back, axis=1, keepdims=True)
        weighted = column * back
        grad_gate = weighted * up_pre * sig * (1.0 + gate_pre * (1.0 - sig))
        grad_up = weighted * act_gate
        grads = jnp.concatenate([grad_gate.astype(BF16), grad_up.astype(BF16)], axis=1)
        return lax.dot_general(grads, pair_ref[...], NT, preferred_element_type=F32), score

    def in_order(score, place, swap_mask):
        token = lax.broadcasted_iota(jnp.int32, (score.shape[0], tokens), 1)
        whole = (place_mask(place // tok, basis) ^ (own ^ swap_mask)) * tok + place % tok
        return jnp.sum(jnp.where(whole == token, score, 0.0), axis=0, keepdims=True)

    half = blocks * rows // 2
    if 2 * half <= 128:
        total, score = terms(own_refs + other_refs, 0, rows)
        kept_ref[...] = total[:half]
        message_ref[:, 0:width] = total[half:].astype(BF16)
        row = lax.broadcasted_iota(jnp.int32, (2 * half, tokens), 0)
        score_ref[...] = in_order(score, row % half, jnp.where(row < half, 0, core_mask))
    else:
        step = min(rows, 128)
        score_ref[...] = jnp.zeros(score_ref.shape, F32)
        for out_ref, sets, swap_mask in ((kept_ref, own_refs, 0), (message_ref, other_refs, core_mask)):
            for j, ref in enumerate(sets):

                def one(index):
                    total, score = terms((ref,), index * step, step)
                    first = pl.multiple_of(j * (rows // 2) + index * (step // 2), step // 2)
                    out_ref[pl.ds(first, step // 2), 0:width] = total.astype(out_ref.dtype)
                    place = lax.broadcasted_iota(jnp.int32, (step // 2, tokens), 0) + first
                    score_ref[...] += in_order(score, place, swap_mask)

                pl.loop(0, rows // step)(one)

    lane_blocks = tokens // LANES
    padded_ref[...] = jnp.zeros(padded_ref.shape, F32)
    value = score_ref[...]
    for piece in range(SCORE_PIECES):
        rounded = value.astype(BF16).astype(F32)
        for b in range(lane_blocks):
            at = piece * lane_blocks + b
            padded_ref[at : at + 1, :] = rounded[:, b * LANES : (b + 1) * LANES]
        value = value - rounded
    pieces_ref[...] = padded_ref[0 : pieces_ref.shape[0], :]
    put_scores(message_ref, padded_ref, width)


def add_kernel(arrivals, positions, *refs):
    kept_ref, pieces_ref = refs[0], refs[1]
    arrived = refs[2 : 2 + arrivals]
    outs = refs[2 + arrivals :]
    next_kept_ref, next_pieces_ref = outs[0], outs[1]
    sends = outs[2 : 2 + len(positions)]
    total_ref, scores_ref = outs[2 + len(positions) :]
    width = kept_ref.shape[1]
    size = pieces_ref.shape[0]
    total = kept_ref[...]
    for ref in arrived:
        total = total + ref[:, 0:width].astype(F32)
    total_ref[...] = total
    if scores_ref.shape[0] > next_pieces_ref.shape[0]:
        scores_ref[...] = jnp.zeros(scores_ref.shape, F32)
    scores_ref[0:size, :] = pieces_ref[...]
    for j, ref in enumerate(arrived):
        get_scores(ref, scores_ref, (j + 1) * size, size, width)
    rows = next_kept_ref.shape[0]
    next_kept_ref[...] = total_ref[0:rows, :]
    next_pieces_ref[...] = scores_ref[0 : next_pieces_ref.shape[0], :]
    for j, ref in zip(positions, sends):
        ref[:, 0:width] = total_ref[j * rows : (j + 1) * rows, :].astype(BF16)
        put_scores(ref, scores_ref, width)


def table_kernel(basis, group, tok, core_mask, rows_out, blocks, after_ref, *refs):
    probs_ref, column_ref, mine_ref = refs[2 * blocks :]
    rows, buf_width = refs[0].shape
    half = blocks * rows // 2
    experts, tokens = probs_ref.shape
    lanes = -(-PIECES * experts // LANES) * LANES
    width = buf_width - lanes
    own = own_index()
    lane = lax.broadcasted_iota(jnp.int32, (experts, lanes), 1)
    ids = lax.broadcasted_iota(jnp.int32, (experts, lanes), 0)
    tally = jnp.zeros((experts, lanes), F32)
    for k in range(1, PIECES):
        tally = tally + jnp.where(lane == ids + k * experts, 1.0, 0.0)
    column = pl.multiple_of(own * rows_out // LANES * LANES, LANES)
    extras = jnp.zeros((tokens, lanes), F32)
    columns = jnp.zeros((tokens, LANES), F32)
    for index in range(2):
        sets = forward(refs[index * blocks : (index + 1) * blocks])
        row = lax.broadcasted_iota(jnp.int32, (half, tokens), 0)
        token = lax.broadcasted_iota(jnp.int32, (half, tokens), 1)
        whole = (place_mask(row // tok, basis) ^ (own ^ (core_mask if index else 0))) * tok + row % tok
        here = jnp.where(whole == token, 1.0, 0.0).astype(BF16)
        part = token_rows(sets, 0, rows, group, 0, slice(width, buf_width))
        extras = extras + lax.dot_general(here, part, TN, preferred_element_type=F32)
        part = token_rows(sets, 0, rows, group, 0, pl.ds(column, LANES))
        columns = columns + lax.dot_general(here, part, TN, preferred_element_type=F32)
    probs_ref[...] = lax.dot_general(tally.astype(BF16), extras.astype(BF16), NT, preferred_element_type=F32)
    column_ref[...] = columns.astype(BF16)
    row = lax.broadcasted_iota(jnp.int32, mine_ref.shape, 0)
    token = lax.broadcasted_iota(jnp.int32, mine_ref.shape, 1)
    mine_ref[...] = jnp.where((row < tok) & (token == own * tok + row), 1.0, 0.0).astype(BF16)


def final_kernel(arrivals, back_basis, *refs):
    probs_ref, column_ref, mine_ref, router_ref, kept_ref, pieces_ref = refs[:6]
    arrived = refs[6 : 6 + arrivals]
    x_out, grad_out, x_ref, grad_ref, scores_ref, sems = refs[6 + arrivals :]
    experts, width = router_ref.shape
    size = pieces_ref.shape[0]
    tok = kept_ref.shape[0]
    own = own_index()
    scores_ref[0:size, :] = pieces_ref[...]
    for j, ref in enumerate(arrived):
        get_scores(ref, scores_ref, (j + 1) * size, size, width)
    blocks = probs_ref.shape[1] // LANES
    wide = scores_ref.shape[0] // blocks
    sender = lax.broadcasted_iota(jnp.int32, (experts, wide), 1) // SCORE_PIECES
    ids = lax.broadcasted_iota(jnp.int32, (experts, wide), 0)
    pick = jnp.where(((place_mask(sender, back_basis) ^ own) >> 1) == ids, 1.0, 0.0).astype(BF16)
    parts = []
    for b in range(blocks):
        block = scores_ref[...] if blocks == 1 else scores_ref[pl.ds(b, wide, stride=blocks), :]
        parts.append(jnp.dot(pick, block.astype(BF16), preferred_element_type=F32))
    scores = parts[0] if blocks == 1 else jnp.concatenate(parts, axis=1)
    probs = probs_ref[...]
    mean = jnp.sum(probs * scores, axis=0, keepdims=True)
    logit_grad = (probs * (scores - mean)).astype(BF16)
    mine = lax.dot_general(mine_ref[...], logit_grad, NT, preferred_element_type=F32)
    part = jnp.dot(mine.astype(BF16), router_ref[...], preferred_element_type=F32)
    total = kept_ref[...]
    for ref in arrived:
        total = total + ref[:, 0:width].astype(F32)
    x_ref[...] = (total + part[:tok]).astype(BF16)
    x_copy = pltpu.make_async_copy(x_ref, x_out, sems.at[0])
    x_copy.start()
    grad = jnp.dot(logit_grad, column_ref[...], preferred_element_type=F32)
    rows_out = grad_ref.shape[1]
    first = own * rows_out % LANES
    grad_ref[...] = pltpu.roll(grad, (LANES - first) % LANES, 1)[:, :rows_out]
    grad_copy = pltpu.make_async_copy(grad_ref, grad_out, sems.at[1])
    grad_copy.start()
    x_copy.wait()
    grad_copy.wait()


def on_device(tokens, grad_out, router_logits, selected, router_w, w_gate, w_up, w_down):
    tok, width = tokens.shape
    experts = router_logits.shape[1]
    hidden = w_gate.shape[2]
    exp_size = lax.axis_size("exp")
    hid_size = lax.axis_size("hid")
    count = exp_size * hid_size
    half = count // 2
    groups, core_mask = stage_masks(exp_size, hid_size)
    basis = [m for group in groups for m in group]
    back_groups = [near_first(group) for group in groups[:0:-1]] + [groups[0]]
    back_basis = [core_mask] + [m for group in back_groups for m in group]
    token_count = count * tok
    lanes = -(-PIECES * experts // LANES) * LANES

    block = pl.pallas_call(
        prep_kernel,
        out_shape=jax.ShapeDtypeStruct((2, tok, width + lanes), BF16),
        in_specs=[HBM_SPEC] * 4,
        out_specs=VMEM_SPEC,
        scratch_shapes=[
            pltpu.VMEM(router_logits.shape, router_logits.dtype),
            pltpu.VMEM(selected.shape, selected.dtype),
            pltpu.SemaphoreType.DMA((4,)),
        ],
        compiler_params=PARAMS,
        name="prep",
    )(*in_hbm(tokens, grad_out, router_logits, selected))

    masks = group_masks(groups[0])
    blocks = [block] + swaps(block, masks[1:], count)
    group_rows = tok * len(blocks)
    block = pl.pallas_call(
        join_kernel,
        out_shape=jax.ShapeDtypeStruct((2 * group_rows, width + lanes), BF16),
        in_specs=[VMEM_SPEC] * len(blocks),
        out_specs=VMEM_SPEC,
        scratch_shapes=[pltpu.VMEM((2 * group_rows, width + lanes), F32)],
        compiler_params=PARAMS,
        name="join",
    )(*forward(blocks))
    for group in groups[1:-1]:
        blocks = [block] + swaps(block, group_masks(group)[1:], count)
        block = pl.pallas_call(
            stack_kernel,
            out_shape=jax.ShapeDtypeStruct((len(blocks) * block.shape[0], block.shape[1]), BF16),
            in_specs=[VMEM_SPEC] * len(blocks),
            out_specs=VMEM_SPEC,
            compiler_params=PARAMS,
            name="stack",
        )(*blocks)
    chunks = 4
    copied, pair, down = pl.pallas_call(
        functools.partial(load_kernel, chunks),
        out_shape=(
            pltpu.VMEM(block.shape, BF16),
            pltpu.VMEM((width, 2 * hidden), BF16),
            pltpu.VMEM((hidden, width), BF16),
        ),
        in_specs=[VMEM_SPEC] + [HBM_SPEC] * 3,
        out_specs=(VMEM_SPEC,) * 3,
        scratch_shapes=[pltpu.SemaphoreType.DMA((3 * chunks + 1,))],
        compiler_params=pltpu.CompilerParams(vmem_limit_bytes=4 * 2**20),
        cost_estimate=pl.CostEstimate(flops=0, bytes_accessed=6 * width * hidden * 2, transcendentals=0),
        name="load",
    )(block, *in_hbm(w_gate, w_up, w_down))
    masks = group_masks(groups[-1]) if len(groups) > 1 else [0]
    blocks = [block] + swaps(block, masks[1:], count)
    blocks = forward(blocks)
    blocks = blocks + [swap(b, core_mask, count) for b in [copied] + blocks[1:]]
    block_count = len(blocks) // 2

    unit_rows = SCORE_PIECES * token_count // LANES
    extra = -(-unit_rows // (half * tok)) * LANES
    kept, message, pieces = pl.pallas_call(
        functools.partial(units_kernel, basis, group_rows, tok, core_mask, block_count),
        out_shape=(
            jax.ShapeDtypeStruct((half * tok, width), F32),
            jax.ShapeDtypeStruct((half * tok, width + extra), BF16),
            jax.ShapeDtypeStruct((unit_rows, LANES), F32),
        ),
        in_specs=[VMEM_SPEC] * (len(blocks) + 2),
        out_specs=(VMEM_SPEC,) * 3,
        scratch_shapes=[
            pltpu.VMEM((1, token_count), F32),
            pltpu.VMEM((max(half * tok * extra // LANES, unit_rows), LANES), F32),
        ],
        compiler_params=PARAMS,
        cost_estimate=pl.CostEstimate(
            flops=10 * token_count * width * hidden,
            bytes_accessed=3 * width * hidden * 2 + 2 * token_count * width * 2,
            transcendentals=token_count * hidden,
        ),
        name="units",
    )(*blocks, pair, down)

    arrived = [swap(message, core_mask, count)]
    tables = None
    rows_out = width // count
    for group, back_group in zip(groups[::-1], back_groups):
        masks = group_masks(group)
        back_masks = group_masks(back_group)
        radix = len(masks)
        rows = kept.shape[0]
        next_rows = rows // radix
        size = pieces.shape[0] * (1 + len(arrived))
        extra = -(-size // next_rows) * LANES
        sends = [jax.ShapeDtypeStruct((next_rows, width + extra), BF16)] * (radix - 1)
        outs = pl.pallas_call(
            functools.partial(add_kernel, len(arrived), [masks.index(m) for m in back_masks[1:]]),
            out_shape=[
                jax.ShapeDtypeStruct((next_rows, width), F32),
                jax.ShapeDtypeStruct((size, LANES), F32),
            ]
            + sends,
            in_specs=[VMEM_SPEC] * (2 + len(arrived)),
            out_specs=[VMEM_SPEC] * (1 + radix),
            scratch_shapes=[
                pltpu.VMEM((rows, width), F32),
                pltpu.VMEM((max(next_rows * extra // LANES, size), LANES), F32),
            ],
            compiler_params=PARAMS,
            name="add",
        )(kept, pieces, *arrived)
        kept, pieces = outs[0], outs[1]
        if tables is None:
            tables = pl.pallas_call(
                functools.partial(table_kernel, basis, group_rows, tok, core_mask, rows_out, block_count),
                out_shape=(
                    jax.ShapeDtypeStruct((experts, token_count), F32),
                    jax.ShapeDtypeStruct((token_count, LANES), BF16),
                    jax.ShapeDtypeStruct((16, token_count), BF16),
                ),
                in_specs=[pl.BlockSpec(memory_space=pl.ANY)] + [VMEM_SPEC] * len(blocks),
                out_specs=(VMEM_SPEC,) * 3,
                compiler_params=PARAMS,
                cost_estimate=pl.CostEstimate(flops=10**9, bytes_accessed=10**6, transcendentals=0),
                name="tables",
            )(pieces, *blocks)
        arrived = [swap(piece, m, count) for piece, m in zip(outs[2:], back_masks[1:])]

    x_grad, grad = pl.pallas_call(
        functools.partial(final_kernel, len(arrived), back_basis),
        out_shape=(
            jax.ShapeDtypeStruct((tok, width), BF16),
            jax.ShapeDtypeStruct((experts, rows_out), F32),
        ),
        in_specs=[VMEM_SPEC] * (6 + len(arrived)),
        out_specs=(HBM_SPEC, HBM_SPEC),
        scratch_shapes=[
            pltpu.VMEM((tok, width), BF16),
            pltpu.VMEM((experts, rows_out), F32),
            pltpu.VMEM((pieces.shape[0] * (1 + len(arrived)), LANES), F32),
            pltpu.SemaphoreType.DMA((2,)),
        ],
        compiler_params=PARAMS,
        name="final",
    )(*tables, router_w.T, kept, pieces, *arrived)
    return (x_grad, grad.T)


def solution(mesh):
    rows = P(AXES, None)
    units = P(AXES, None, None)
    return jax.shard_map(
        on_device,
        mesh=mesh,
        in_specs=(rows, rows, rows, rows, P(), units, units, units),
        out_specs=(rows, rows),
        check_vma=False,
    )
```

profile of v0, /device:TPU:0, one launch (start us, length us, event | category | flops | bytes accessed | tf_op | source)
XLA Modules:
  0.0 40.4 jit_solution(5060480713970419423)
XLA Ops:
  0.6 1.0 %prep.1.refs_0_ = bf16[2,4,2176]{2,1,0:T(4,128)(2,1)S(1)} custom-call(bf16[4,2048]{1,0:T(4,128)(2,1)} %tokens_in.1, bf16[4,2048]{1,0:T(4,128)(2,1)} %grad_in.1, f32[4,16]{1,0:T(4,128)} %logits_in.1, s32[4,8]{1,0:T(4,128)} %chosen_in.1), custom_call_target="tpu_custom_call" | custom-call | tf_op jit(solution)/shard_map/prep/pallas_call | solution.py:361
  1.6 5.1 %collective-permute-start.2 = (bf16[2,4,2176]{2,1,0:T(4,128)(2,1)S(1)}, bf16[2,4,2176]{2,1,0:T(4,128)(2,1)S(1)}, u32[]{:S(2)}, u32[]{:S(2)}) collective-permute-start(bf16[2,4,2176]{2,1,0:T(4,128)(2,1)S(1)} %prep.1.refs_0_), channel_id=1, source_target_pairs={{0,24},{1,25},{2,26},{3,27},{4,28},{5,29},{6,30},{7,31},{8,16},{9,... | collective-permute-start | bytes 104456 | tf_op jit(solution)/shard_map/ppermute | solution.py:46
  6.8 0.6 %collective-permute-start = (bf16[2,4,2176]{2,1,0:T(4,128)(2,1)S(1)}, bf16[2,4,2176]{2,1,0:T(4,128)(2,1)S(1)}, u32[]{:S(2)}, u32[]{:S(2)}) collective-permute-start(bf16[2,4,2176]{2,1,0:T(4,128)(2,1)S(1)} %prep.1.refs_0_), channel_id=1, source_target_pairs={{0,8},{1,9},{2,10},{3,11},{4,12},{5,13},{6,14},{7,15},{8,0},{9,1},... | collective-permute-start | bytes 104456 | tf_op jit(solution)/shard_map/ppermute | solution.py:46
  7.4 1.3 %collective-permute-done.2.refs_3_ = bf16[2,4,2176]{2,1,0:T(4,128)(2,1)S(1)} collective-permute-done((bf16[2,4,2176]{2,1,0:T(4,128)(2,1)S(1)}, bf16[2,4,2176]{2,1,0:T(4,128)(2,1)S(1)}, u32[]{:S(2)}, u32[]{:S(2)}) %collective-permute-start.2) | collective-permute-done | bytes 34848 | tf_op jit(solution)/shard_map/ppermute | solution.py:46
  8.7 2.9 %collective-permute-done.1.refs_2_ = bf16[2,4,2176]{2,1,0:T(4,128)(2,1)S(1)} collective-permute-done((bf16[2,4,2176]{2,1,0:T(4,128)(2,1)S(1)}, bf16[2,4,2176]{2,1,0:T(4,128)(2,1)S(1)}, u32[]{:S(2)}, u32[]{:S(2)}) %collective-permute-start.1) | collective-permute-done | bytes 34848 | tf_op jit(solution)/shard_map/ppermute | solution.py:46
  11.6 2.5 %collective-permute-start.5 = (bf16[32,2176]{1,0:T(8,128)(2,1)S(1)}, bf16[32,2176]{1,0:T(8,128)(2,1)S(1)}, u32[]{:S(2)}, u32[]{:S(2)}) collective-permute-start(bf16[32,2176]{1,0:T(8,128)(2,1)S(1)} %join.1.block_in.refs_0_), channel_id=1, source_target_pairs={{0,5},{1,4},{2,7},{3,6},{4,1},{5,0},{6,3},{7,2},{8,13},{9,12},{10,... | collective-permute-start | bytes 417800 | tf_op jit(solution)/shard_map/ppermute | solution.py:46
  14.2 0.5 %collective-permute-start.4 = (bf16[32,2176]{1,0:T(8,128)(2,1)S(1)}, bf16[32,2176]{1,0:T(8,128)(2,1)S(1)}, u32[]{:S(2)}, u32[]{:S(2)}) collective-permute-start(bf16[32,2176]{1,0:T(8,128)(2,1)S(1)} %join.1.block_in.refs_0_), channel_id=1, source_target_pairs={{0,4},{1,5},{2,6},{3,7},{4,0},{5,1},{6,2},{7,3},{8,12},{9,13},{10,... | collective-permute-start | bytes 417800 | tf_op jit(solution)/shard_map/ppermute | solution.py:46
  14.7 0.5 %collective-permute-start.3 = (bf16[32,2176]{1,0:T(8,128)(2,1)S(1)}, bf16[32,2176]{1,0:T(8,128)(2,1)S(1)}, u32[]{:S(2)}, u32[]{:S(2)}) collective-permute-start(bf16[32,2176]{1,0:T(8,128)(2,1)S(1)} %join.1.block_in.refs_0_), channel_id=1, source_target_pairs={{0,1},{1,0},{2,3},{3,2},{4,5},{5,4},{6,7},{7,6},{8,9},{9,8},{10,11... | collective-permute-start | bytes 417800 | tf_op jit(solution)/shard_map/ppermute | solution.py:46
  15.2 2.4 %load.1 = (bf16[32,2176]{1,0:T(8,128)(2,1)S(1)}, bf16[2048,768]{1,0:T(8,128)(2,1)S(1)}, bf16[384,2048]{1,0:T(8,128)(2,1)S(1)}) custom-call(bf16[32,2176]{1,0:T(8,128)(2,1)S(1)} %join.1.block_in.refs_0_, bf16[1,2048,384]{2,1,0:T(8,128)(2,1)} %gate_in.1, bf16[1,2048,384]{2,1,0:T(8,128)(2,1)} %up_in.1, bf16[1,384,2048]{2,1,0:T(8,128)(2,1)} %down_in.1), custom_call_target="tpu_custom_call" | custom-call | bytes 9437184 | tf_op jit(solution)/shard_map/load/pallas_call | solution.py:398
  17.6 0.1 collective-permute-start.6
  17.7 1.5 %collective-permute-done.5.refs_3_ = bf16[32,2176]{1,0:T(8,128)(2,1)S(1)} collective-permute-done((bf16[32,2176]{1,0:T(8,128)(2,1)S(1)}, bf16[32,2176]{1,0:T(8,128)(2,1)S(1)}, u32[]{:S(2)}, u32[]{:S(2)}) %collective-permute-start.5) | collective-permute-done | bytes 139296 | tf_op jit(solution)/shard_map/ppermute | solution.py:46
  19.2 0.8 %collective-permute-done.4.refs_2_ = bf16[32,2176]{1,0:T(8,128)(2,1)S(1)} collective-permute-done((bf16[32,2176]{1,0:T(8,128)(2,1)S(1)}, bf16[32,2176]{1,0:T(8,128)(2,1)S(1)}, u32[]{:S(2)}, u32[]{:S(2)}) %collective-permute-start.4) | collective-permute-done | bytes 139296 | tf_op jit(solution)/shard_map/ppermute | solution.py:46
  19.9 0.5 %collective-permute-start.7 = (bf16[32,2176]{1,0:T(8,128)(2,1)S(1)}, bf16[32,2176]{1,0:T(8,128)(2,1)S(1)}, u32[]{:S(2)}, u32[]{:S(2)}) collective-permute-start(bf16[32,2176]{1,0:T(8,128)(2,1)S(1)} %collective-permute-done.3.refs_1_), channel_id=1, source_target_pairs={{0,2},{1,3},{2,0},{3,1},{4,6},{5,7},{6,4},{7,5},{8,10},{9,11},{10,... | collective-permute-start | bytes 417800 | tf_op jit(solution)/shard_map/ppermute | solution.py:46
  20.5 0.8 %collective-permute-done.8.refs_6_ = bf16[32,2176]{1,0:T(8,128)(2,1)S(1)} collective-permute-done((bf16[32,2176]{1,0:T(8,128)(2,1)S(1)}, bf16[32,2176]{1,0:T(8,128)(2,1)S(1)}, u32[]{:S(2)}, u32[]{:S(2)}) %collective-permute-start.8) | collective-permute-done | bytes 139296 | tf_op jit(solution)/shard_map/ppermute | solution.py:46
  21.3 0.2 collective-permute-done.7.refs_5_
  21.5 2.1 %units.1 = (f32[64,2048]{1,0:T(8,128)S(1)}, bf16[64,2176]{1,0:T(8,128)(2,1)S(1)}, f32[2,128]{1,0:T(2,128)S(1)}) custom-call(bf16[32,2176]{1,0:T(8,128)(2,1)S(1)} %join.1.block_in.refs_0_, bf16[32,2176]{1,0:T(8,128)(2,1)S(1)} %collective-permute-done.3.refs_1_, bf16[32,2176]{1,0:T(8,128)(2,1)S(1)} %collective-permute-done.4.refs_2_, ...), custom_call_target="tpu_custom_call" | custom-call | flops 1006632960 | bytes 5767168 | tf_op jit(solution)/shard_map/units/pallas_call | solution.py:420
  23.6 0.4 collective-permute-start.10
  24.0 1.2 %collective-permute-done.10.refs_2_ = bf16[64,2176]{1,0:T(8,128)(2,1)S(1)} collective-permute-done((bf16[64,2176]{1,0:T(8,128)(2,1)S(1)}, bf16[64,2176]{1,0:T(8,128)(2,1)S(1)}, u32[]{:S(2)}, u32[]{:S(2)}) %collective-permute-start.10) | collective-permute-done | bytes 278560 | tf_op jit(solution)/shard_map/ppermute | solution.py:46
  25.2 0.1 add.2
  25.3 1.2 %collective-permute-start.11 = (bf16[16,2176]{1,0:T(8,128)(2,1)S(1)}, bf16[16,2176]{1,0:T(8,128)(2,1)S(1)}, u32[]{:S(2)}, u32[]{:S(2)}) collective-permute-start(bf16[16,2176]{1,0:T(8,128)(2,1)S(1)} %get-tuple-element.34), channel_id=1, source_target_pairs={{0,1},{1,0},{2,3},{3,2},{4,5},{5,4},{6,7},{7,6},{8,9},{9,8},{10,11... | collective-permute-start | bytes 208904 | tf_op jit(solution)/shard_map/ppermute | solution.py:46
  26.5 0.8 %collective-permute-start.12 = (bf16[16,2176]{1,0:T(8,128)(2,1)S(1)}, bf16[16,2176]{1,0:T(8,128)(2,1)S(1)}, u32[]{:S(2)}, u32[]{:S(2)}) collective-permute-start(bf16[16,2176]{1,0:T(8,128)(2,1)S(1)} %get-tuple-element.35), channel_id=1, source_target_pairs={{0,4},{1,5},{2,6},{3,7},{4,0},{5,1},{6,2},{7,3},{8,12},{9,13},{10,... | collective-permute-start | bytes 208904 | tf_op jit(solution)/shard_map/ppermute | solution.py:46
  27.3 1.5 %collective-permute-start.13 = (bf16[16,2176]{1,0:T(8,128)(2,1)S(1)}, bf16[16,2176]{1,0:T(8,128)(2,1)S(1)}, u32[]{:S(2)}, u32[]{:S(2)}) collective-permute-start(bf16[16,2176]{1,0:T(8,128)(2,1)S(1)} %get-tuple-element.36), channel_id=1, source_target_pairs={{0,5},{1,4},{2,7},{3,6},{4,1},{5,0},{6,3},{7,2},{8,13},{9,12},{10,... | collective-permute-start | bytes 208904 | tf_op jit(solution)/shard_map/ppermute | solution.py:46
  28.9 0.9 %collective-permute-done.11.refs_2_ = bf16[16,2176]{1,0:T(8,128)(2,1)S(1)} collective-permute-done((bf16[16,2176]{1,0:T(8,128)(2,1)S(1)}, bf16[16,2176]{1,0:T(8,128)(2,1)S(1)}, u32[]{:S(2)}, u32[]{:S(2)}) %collective-permute-start.11) | collective-permute-done | bytes 69664 | tf_op jit(solution)/shard_map/ppermute | solution.py:46
  29.8 1.8 %collective-permute-done.12.refs_3_ = bf16[16,2176]{1,0:T(8,128)(2,1)S(1)} collective-permute-done((bf16[16,2176]{1,0:T(8,128)(2,1)S(1)}, bf16[16,2176]{1,0:T(8,128)(2,1)S(1)}, u32[]{:S(2)}, u32[]{:S(2)}) %collective-permute-start.12) | collective-permute-done | bytes 69664 | tf_op jit(solution)/shard_map/ppermute | solution.py:46
  31.6 1.0 %collective-permute-done.13.refs_4_ = bf16[16,2176]{1,0:T(8,128)(2,1)S(1)} collective-permute-done((bf16[16,2176]{1,0:T(8,128)(2,1)S(1)}, bf16[16,2176]{1,0:T(8,128)(2,1)S(1)}, u32[]{:S(2)}, u32[]{:S(2)}) %collective-permute-start.13) | collective-permute-done | bytes 69664 | tf_op jit(solution)/shard_map/ppermute | solution.py:46
  32.6 2.0 %collective-permute-start.14 = (bf16[4,2560]{1,0:T(4,128)(2,1)S(1)}, bf16[4,2560]{1,0:T(4,128)(2,1)S(1)}, u32[]{:S(2)}, u32[]{:S(2)}) collective-permute-start(bf16[4,2560]{1,0:T(4,128)(2,1)S(1)} %get-tuple-element.39), channel_id=1, source_target_pairs={{0,24},{1,25},{2,26},{3,27},{4,28},{5,29},{6,30},{7,31},{8,16},{9,... | collective-permute-start | bytes 61448 | tf_op jit(solution)/shard_map/ppermute | solution.py:46
  34.6 0.2 collective-permute-start.15
  34.8 2.3 %collective-permute-start.16 = (bf16[4,2560]{1,0:T(4,128)(2,1)S(1)}, bf16[4,2560]{1,0:T(4,128)(2,1)S(1)}, u32[]{:S(2)}, u32[]{:S(2)}) collective-permute-start(bf16[4,2560]{1,0:T(4,128)(2,1)S(1)} %get-tuple-element.41), channel_id=1, source_target_pairs={{0,8},{1,9},{2,10},{3,11},{4,12},{5,13},{6,14},{7,15},{8,0},{9,1},... | collective-permute-start | bytes 61448 | tf_op jit(solution)/shard_map/ppermute | solution.py:46
  37.1 0.4 tables.1
  37.4 0.8 %collective-permute-done.14.refs_6_ = bf16[4,2560]{1,0:T(4,128)(2,1)S(1)} collective-permute-done((bf16[4,2560]{1,0:T(4,128)(2,1)S(1)}, bf16[4,2560]{1,0:T(4,128)(2,1)S(1)}, u32[]{:S(2)}, u32[]{:S(2)}) %collective-permute-start.14) | collective-permute-done | bytes 20512 | tf_op jit(solution)/shard_map/ppermute | solution.py:46
  38.3 1.0 %collective-permute-done.15.refs_7_ = bf16[4,2560]{1,0:T(4,128)(2,1)S(1)} collective-permute-done((bf16[4,2560]{1,0:T(4,128)(2,1)S(1)}, bf16[4,2560]{1,0:T(4,128)(2,1)S(1)}, u32[]{:S(2)}, u32[]{:S(2)}) %collective-permute-start.15) | collective-permute-done | bytes 20512 | tf_op jit(solution)/shard_map/ppermute | solution.py:46
  39.3 1.1 %final.1 = (bf16[4,2048]{1,0:T(4,128)(2,1)}, f32[16,64]{1,0:T(8,128)}) custom-call(f32[16,128]{1,0:T(8,128)S(1)} %get-tuple-element.30.refs_0_, bf16[128,128]{1,0:T(8,128)(2,1)S(1)} %get-tuple-element.31.refs_1_, bf16[16,128]{1,0:T(8,128)(2,1)S(1)} %get-tuple-element.32.refs_2_, bf16[16,2048]{1,0:T(8,128)(2,1)S(1)} %bitcast.2, ...), custom_call_target="tpu_custom_call" | custom-call | tf_op jit(solution)/shard_map/final/pallas_call | solution.py:487
  (12 shorter events, 0.2 us)
Async XLA Ops:
  1.6 7.0 %collective-permute-start.2 = (bf16[2,4,2176]{2,1,0:T(4,128)(2,1)S(1)}, bf16[2,4,2176]{2,1,0:T(4,128)(2,1)S(1)}, u32[]{:S(2)}, u32[]{:S(2)}) collective-permute-start(bf16[2,4,2176]{2,1,0:T(4,128)(2,1)S(1)} %prep.1.refs_0_), channel_id=1, source_target_pairs={{0,24},{1,25},{2,26},{3,27},{4,28},{5,29},{6,30},{7,31},{8,16},{9,... | collective-permute-start | bytes 104456 | tf_op jit(solution)/shard_map/ppermute | solution.py:46
  6.8 4.8 %collective-permute-start.1 = (bf16[2,4,2176]{2,1,0:T(4,128)(2,1)S(1)}, bf16[2,4,2176]{2,1,0:T(4,128)(2,1)S(1)}, u32[]{:S(2)}, u32[]{:S(2)}) collective-permute-start(bf16[2,4,2176]{2,1,0:T(4,128)(2,1)S(1)} %prep.1.refs_0_), channel_id=1, source_target_pairs={{0,16},{1,17},{2,18},{3,19},{4,20},{5,21},{6,22},{7,23},{8,24},{9,... | collective-permute-start | bytes 104456 | tf_op jit(solution)/shard_map/ppermute | solution.py:46
  6.8 4.8 %collective-permute-start = (bf16[2,4,2176]{2,1,0:T(4,128)(2,1)S(1)}, bf16[2,4,2176]{2,1,0:T(4,128)(2,1)S(1)}, u32[]{:S(2)}, u32[]{:S(2)}) collective-permute-start(bf16[2,4,2176]{2,1,0:T(4,128)(2,1)S(1)} %prep.1.refs_0_), channel_id=1, source_target_pairs={{0,8},{1,9},{2,10},{3,11},{4,12},{5,13},{6,14},{7,15},{8,0},{9,1},... | collective-permute-start | bytes 104456 | tf_op jit(solution)/shard_map/ppermute | solution.py:46
  11.6 7.5 %collective-permute-start.5 = (bf16[32,2176]{1,0:T(8,128)(2,1)S(1)}, bf16[32,2176]{1,0:T(8,128)(2,1)S(1)}, u32[]{:S(2)}, u32[]{:S(2)}) collective-permute-start(bf16[32,2176]{1,0:T(8,128)(2,1)S(1)} %join.1.block_in.refs_0_), channel_id=1, source_target_pairs={{0,5},{1,4},{2,7},{3,6},{4,1},{5,0},{6,3},{7,2},{8,13},{9,12},{10,... | collective-permute-start | bytes 417800 | tf_op jit(solution)/shard_map/ppermute | solution.py:46
  14.2 5.8 %collective-permute-start.4 = (bf16[32,2176]{1,0:T(8,128)(2,1)S(1)}, bf16[32,2176]{1,0:T(8,128)(2,1)S(1)}, u32[]{:S(2)}, u32[]{:S(2)}) collective-permute-start(bf16[32,2176]{1,0:T(8,128)(2,1)S(1)} %join.1.block_in.refs_0_), channel_id=1, source_target_pairs={{0,4},{1,5},{2,6},{3,7},{4,0},{5,1},{6,2},{7,3},{8,12},{9,13},{10,... | collective-permute-start | bytes 417800 | tf_op jit(solution)/shard_map/ppermute | solution.py:46
  14.7 5.3 %collective-permute-start.3 = (bf16[32,2176]{1,0:T(8,128)(2,1)S(1)}, bf16[32,2176]{1,0:T(8,128)(2,1)S(1)}, u32[]{:S(2)}, u32[]{:S(2)}) collective-permute-start(bf16[32,2176]{1,0:T(8,128)(2,1)S(1)} %join.1.block_in.refs_0_), channel_id=1, source_target_pairs={{0,1},{1,0},{2,3},{3,2},{4,5},{5,4},{6,7},{7,6},{8,9},{9,8},{10,11... | collective-permute-start | bytes 417800 | tf_op jit(solution)/shard_map/ppermute | solution.py:46
  17.6 2.8 %collective-permute-start.6 = (bf16[32,2176]{1,0:T(8,128)(2,1)S(1)}, bf16[32,2176]{1,0:T(8,128)(2,1)S(1)}, u32[]{:S(2)}, u32[]{:S(2)}) collective-permute-start(bf16[32,2176]{1,0:T(8,128)(2,1)S(1)} %get-tuple-element.23), channel_id=1, source_target_pairs={{0,2},{1,3},{2,0},{3,1},{4,6},{5,7},{6,4},{7,5},{8,10},{9,11},{10,... | collective-permute-start | bytes 417800 | tf_op jit(solution)/shard_map/ppermute | solution.py:46
  19.2 1.4 %collective-permute-start.9 = (bf16[32,2176]{1,0:T(8,128)(2,1)S(1)}, bf16[32,2176]{1,0:T(8,128)(2,1)S(1)}, u32[]{:S(2)}, u32[]{:S(2)}) collective-permute-start(bf16[32,2176]{1,0:T(8,128)(2,1)S(1)} %collective-permute-done.5.refs_3_), channel_id=1, source_target_pairs={{0,2},{1,3},{2,0},{3,1},{4,6},{5,7},{6,4},{7,5},{8,10},{9,11},{10,... | collective-permute-start | bytes 417800 | tf_op jit(solution)/shard_map/ppermute | solution.py:46
  19.9 1.4 %collective-permute-start.8 = (bf16[32,2176]{1,0:T(8,128)(2,1)S(1)}, bf16[32,2176]{1,0:T(8,128)(2,1)S(1)}, u32[]{:S(2)}, u32[]{:S(2)}) collective-permute-start(bf16[32,2176]{1,0:T(8,128)(2,1)S(1)} %collective-permute-done.4.refs_2_), channel_id=1, source_target_pairs={{0,2},{1,3},{2,0},{3,1},{4,6},{5,7},{6,4},{7,5},{8,10},{9,11},{10,... | collective-permute-start | bytes 417800 | tf_op jit(solution)/shard_map/ppermute | solution.py:46
  19.9 1.6 %collective-permute-start.7 = (bf16[32,2176]{1,0:T(8,128)(2,1)S(1)}, bf16[32,2176]{1,0:T(8,128)(2,1)S(1)}, u32[]{:S(2)}, u32[]{:S(2)}) collective-permute-start(bf16[32,2176]{1,0:T(8,128)(2,1)S(1)} %collective-permute-done.3.refs_1_), channel_id=1, source_target_pairs={{0,2},{1,3},{2,0},{3,1},{4,6},{5,7},{6,4},{7,5},{8,10},{9,11},{10,... | collective-permute-start | bytes 417800 | tf_op jit(solution)/shard_map/ppermute | solution.py:46
  23.6 1.6 %collective-permute-start.10 = (bf16[64,2176]{1,0:T(8,128)(2,1)S(1)}, bf16[64,2176]{1,0:T(8,128)(2,1)S(1)}, u32[]{:S(2)}, u32[]{:S(2)}) collective-permute-start(bf16[64,2176]{1,0:T(8,128)(2,1)S(1)} %get-tuple-element.28), channel_id=1, source_target_pairs={{0,2},{1,3},{2,0},{3,1},{4,6},{5,7},{6,4},{7,5},{8,10},{9,11},{10,... | collective-permute-start | bytes 835592 | tf_op jit(solution)/shard_map/ppermute | solution.py:46
  25.3 4.5 %collective-permute-start.11 = (bf16[16,2176]{1,0:T(8,128)(2,1)S(1)}, bf16[16,2176]{1,0:T(8,128)(2,1)S(1)}, u32[]{:S(2)}, u32[]{:S(2)}) collective-permute-start(bf16[16,2176]{1,0:T(8,128)(2,1)S(1)} %get-tuple-element.34), channel_id=1, source_target_pairs={{0,1},{1,0},{2,3},{3,2},{4,5},{5,4},{6,7},{7,6},{8,9},{9,8},{10,11... | collective-permute-start | bytes 208904 | tf_op jit(solution)/shard_map/ppermute | solution.py:46
  26.5 5.1 %collective-permute-start.12 = (bf16[16,2176]{1,0:T(8,128)(2,1)S(1)}, bf16[16,2176]{1,0:T(8,128)(2,1)S(1)}, u32[]{:S(2)}, u32[]{:S(2)}) collective-permute-start(bf16[16,2176]{1,0:T(8,128)(2,1)S(1)} %get-tuple-element.35), channel_id=1, source_target_pairs={{0,4},{1,5},{2,6},{3,7},{4,0},{5,1},{6,2},{7,3},{8,12},{9,13},{10,... | collective-permute-start | bytes 208904 | tf_op jit(solution)/shard_map/ppermute | solution.py:46
  27.3 5.2 %collective-permute-start.13 = (bf16[16,2176]{1,0:T(8,128)(2,1)S(1)}, bf16[16,2176]{1,0:T(8,128)(2,1)S(1)}, u32[]{:S(2)}, u32[]{:S(2)}) collective-permute-start(bf16[16,2176]{1,0:T(8,128)(2,1)S(1)} %get-tuple-element.36), channel_id=1, source_target_pairs={{0,5},{1,4},{2,7},{3,6},{4,1},{5,0},{6,3},{7,2},{8,13},{9,12},{10,... | collective-permute-start | bytes 208904 | tf_op jit(solution)/shard_map/ppermute | solution.py:46
  32.6 5.6 %collective-permute-start.14 = (bf16[4,2560]{1,0:T(4,128)(2,1)S(1)}, bf16[4,2560]{1,0:T(4,128)(2,1)S(1)}, u32[]{:S(2)}, u32[]{:S(2)}) collective-permute-start(bf16[4,2560]{1,0:T(4,128)(2,1)S(1)} %get-tuple-element.39), channel_id=1, source_target_pairs={{0,24},{1,25},{2,26},{3,27},{4,28},{5,29},{6,30},{7,31},{8,16},{9,... | collective-permute-start | bytes 61448 | tf_op jit(solution)/shard_map/ppermute | solution.py:46
  34.6 4.7 %collective-permute-start.15 = (bf16[4,2560]{1,0:T(4,128)(2,1)S(1)}, bf16[4,2560]{1,0:T(4,128)(2,1)S(1)}, u32[]{:S(2)}, u32[]{:S(2)}) collective-permute-start(bf16[4,2560]{1,0:T(4,128)(2,1)S(1)} %get-tuple-element.40), channel_id=1, source_target_pairs={{0,16},{1,17},{2,18},{3,19},{4,20},{5,21},{6,22},{7,23},{8,24},{9,... | collective-permute-start | bytes 61448 | tf_op jit(solution)/shard_map/ppermute | solution.py:46
  34.8 4.5 %copy-start = (bf16[2048,16]{0,1:T(8,128)(2,1)S(1)}, bf16[2048,16]{0,1:T(8,128)(2,1)}, u32[]{:S(2)}) copy-start(bf16[2048,16]{0,1:T(8,128)(2,1)} %param.12) | copy-start | bytes 196612
  34.8 4.5 %collective-permute-start.16 = (bf16[4,2560]{1,0:T(4,128)(2,1)S(1)}, bf16[4,2560]{1,0:T(4,128)(2,1)S(1)}, u32[]{:S(2)}, u32[]{:S(2)}) collective-permute-start(bf16[4,2560]{1,0:T(4,128)(2,1)S(1)} %get-tuple-element.41), channel_id=1, source_target_pairs={{0,8},{1,9},{2,10},{3,11},{4,12},{5,13},{6,14},{7,15},{8,0},{9,1},... | collective-permute-start | bytes 61448 | tf_op jit(solution)/shard_map/ppermute | solution.py:46
where the time goes:
time: 40.6 us; the launch traced here: 40.4 us
  starting transfers between devices  18.3 us (45%)
  waiting for transfers between devices  14.2 us (35%)
  Pallas kernels  7.18 us (18%)
  between operations  0.69 us (2%)
    ppermute x17, starting transfers between devices, swap(): return lax.ppermute(block, AXES, [(i, i ^ mask) for i in range(count)])  18.3 us
    ppermute x17, waiting for transfers between devices, swap(): return lax.ppermute(block, AXES, [(i, i ^ mask) for i in range(count)])  14.2 us
    pallas_call x1, Pallas kernels, on_device(): pl.pallas_call(functools.partial(load_kernel, chunks), out_shape=(pltpu.V...  2.41 us
    pallas_call x1, Pallas kernels, on_device(): pl.pallas_call(functools.partial(units_kernel, basis, group_rows, tok, co...  2.12 us
    pallas_call x1, Pallas kernels, on_device(): pl.pallas_call(functools.partial(final_kernel, len(arrived), back_basis),...  1.1 us
    pallas_call x1, Pallas kernels, on_device(): pl.pallas_call(prep_kernel, out_shape=jax.ShapeDtypeStruct((2, tok, width...  1 us
  transfers between devices with their start and end apart: 17, of which 13 were waited for; matrix products, arithmetic and copies ran while one was open for 0% of the time, Pallas kernels for 7%

commit v1 on v0

--- a/solution.py
+++ b/solution.py
@@ -38,8 +38,8 @@
     return masks
 
 
-def near_first(basis):
-    return [a ^ b for a, b in zip(basis, basis[1:] + [0])]
+def nearest_first(basis):
+    return [basis[0] ^ basis[1], basis[0]] if len(basis) == 2 else basis
 
 
 def swap(block, mask, count):
@@ -110,6 +110,11 @@
     copies[3].wait()
 
 
+def hidden_parts(hidden):
+    main = hidden // 256 * 256
+    return [(0, main), (main, hidden)] if 0 < main < hidden else [(0, hidden)]
+
+
 def load_kernel(chunks, block_in, gate_in, up_in, down_in, block_ref, pair_ref, down_ref, sems):
     copies = []
 
@@ -119,8 +124,10 @@
     hidden, width = down_ref.shape
     for c in range(chunks):
         part = pl.ds(c * (width // chunks), width // chunks)
-        add(gate_in.at[0, part, :], pair_ref.at[part, 0:hidden])
-        add(up_in.at[0, part, :], pair_ref.at[part, hidden : 2 * hidden])
+        for first, last in hidden_parts(hidden):
+            for k, ref in enumerate((gate_in, up_in)):
+                to = 2 * first + k * (last - first)
+                add(ref.at[0, part, first:last], pair_ref.at[part, to : to + last - first])
         part = pl.ds(c * (hidden // chunks), hidden // chunks)
         add(down_in.at[0, part, :], down_ref.at[part, :])
     add(block_in, block_ref)
@@ -188,18 +195,24 @@
         extras = act[:, width:].astype(F32)
         lane = lax.broadcasted_iota(jnp.int32, (count, buf_width - width), 1)
         column = jnp.sum(jnp.where(lane == own // 2, extras, 0.0), axis=1, keepdims=True)
-        pair = jnp.dot(act[:, :width], pair_ref[...], preferred_element_type=F32)
-        gate_pre = pair[:, :hidden]
-        up_pre = pair[:, hidden:]
+        act = act[:, :width]
         cot = token_rows(sets, start, step, group, 1, slice(0, width))
-        back = lax.dot_general(cot, down_ref[...], NT, preferred_element_type=F32)
-        sig = jax.nn.sigmoid(gate_pre)
-        act_gate = gate_pre * sig
-        score = jnp.sum(act_gate * up_pre * back, axis=1, keepdims=True)
-        weighted = column * back
-        grad_gate = weighted * up_pre * sig * (1.0 + gate_pre * (1.0 - sig))
-        grad_up = weighted * act_gate
-        grads = jnp.concatenate([grad_gate.astype(BF16), grad_up.astype(BF16)], axis=1)
+        score = jnp.zeros((count, 1), F32)
+        grads = []
+        for first, last in hidden_parts(hidden):
+            size = last - first
+            pair = jnp.dot(act, pair_ref[:, 2 * first : 2 * last], preferred_element_type=F32)
+            gate_pre = pair[:, :size]
+            up_pre = pair[:, size:]
+            back = lax.dot_general(cot, down_ref[first:last, :], NT, preferred_element_type=F32)
+            sig = jax.nn.sigmoid(gate_pre)
+            act_gate = gate_pre * sig
+            score = score + jnp.sum(act_gate * up_pre * back, axis=1, keepdims=True)
+            weighted = column * back
+            grad_gate = weighted * up_pre * sig * (1.0 + gate_pre * (1.0 - sig))
+            grad_up = weighted * act_gate
+            grads += [grad_gate.astype(BF16), grad_up.astype(BF16)]
+        grads = jnp.concatenate(grads, axis=1)
         return lax.dot_general(grads, pair_ref[...], NT, preferred_element_type=F32), score
 
     def in_order(score, place, swap_mask):
@@ -353,7 +366,7 @@
     half = count // 2
     groups, core_mask = stage_masks(exp_size, hid_size)
     basis = [m for group in groups for m in group]
-    back_groups = [near_first(group) for group in groups[:0:-1]] + [groups[0]]
+    back_groups = [nearest_first(group) for group in groups[:0:-1]] + [groups[0]]
     back_basis = [core_mask] + [m for group in back_groups for m in group]
     token_count = count * tok
     lanes = -(-PIECES * experts // LANES) * LANES
@@ -404,7 +417,7 @@
         ),
         in_specs=[VMEM_SPEC] + [HBM_SPEC] * 3,
         out_specs=(VMEM_SPEC,) * 3,
-        scratch_shapes=[pltpu.SemaphoreType.DMA((3 * chunks + 1,))],
+        scratch_shapes=[pltpu.SemaphoreType.DMA(((2 * len(hidden_parts(hidden)) + 1) * chunks + 1,))],
         compiler_params=pltpu.CompilerParams(vmem_limit_bytes=4 * 2**20),
         cost_estimate=pl.CostEstimate(flops=0, bytes_accessed=6 * width * hidden * 2, transcendentals=0),
         name="load",

time: 40.6 us -> 41.1 us (1.012)
  waiting for transfers between devices: 14.2 us -> 14.7 us
    ppermute x17, waiting for transfers between devices: 14.2 us -> 14.7 us  [swap(): return lax.ppermute(block, AXES, [(i, i ^ mask) for i in range(count)])]
where the time goes in v1:
time: 41.1 us; the launch traced here: 40.9 us
  starting transfers between devices  18.3 us (45%)
  waiting for transfers between devices  14.7 us (36%)
  Pallas kernels  7.23 us (18%)
  between operations  0.69 us (2%)
    ppermute x17, starting transfers between devices, swap(): return lax.ppermute(block, AXES, [(i, i ^ mask) for i in range(count)])  18.3 us
    ppermute x17, waiting for transfers between devices, swap(): return lax.ppermute(block, AXES, [(i, i ^ mask) for i in range(count)])  14.7 us
    pallas_call x1, Pallas kernels, on_device(): pl.pallas_call(functools.partial(load_kernel, chunks), out_shape=(pltpu.V...  2.48 us
    pallas_call x1, Pallas kernels, on_device(): pl.pallas_call(functools.partial(units_kernel, basis, group_rows, tok, co...  2.1 us
    pallas_call x1, Pallas kernels, on_device(): pl.pallas_call(functools.partial(final_kernel, len(arrived), back_basis),...  1.1 us
    pallas_call x1, Pallas kernels, on_device(): pl.pallas_call(prep_kernel, out_shape=jax.ShapeDtypeStruct((2, tok, width...  1 us
  transfers between devices with their start and end apart: 17, of which 13 were waited for; matrix products, arithmetic and copies ran while one was open for 0% of the time, Pallas kernels for 7%

profile of v1, /device:TPU:0, one launch (start us, length us, event | category | flops | bytes accessed | tf_op | source)
XLA Modules:
  0.0 40.9 jit_solution(2582129786495753254)
XLA Ops:
  0.6 1.0 %prep.1.refs_0_ = bf16[2,4,2176]{2,1,0:T(4,128)(2,1)S(1)} custom-call(bf16[4,2048]{1,0:T(4,128)(2,1)} %tokens_in.1, bf16[4,2048]{1,0:T(4,128)(2,1)} %grad_in.1, f32[4,16]{1,0:T(4,128)} %logits_in.1, s32[4,8]{1,0:T(4,128)} %chosen_in.1), custom_call_target="tpu_custom_call" | custom-call | tf_op jit(solution)/shard_map/prep/pallas_call | solution.py:374
  1.6 5.1 %collective-permute-start.2 = (bf16[2,4,2176]{2,1,0:T(4,128)(2,1)S(1)}, bf16[2,4,2176]{2,1,0:T(4,128)(2,1)S(1)}, u32[]{:S(2)}, u32[]{:S(2)}) collective-permute-start(bf16[2,4,2176]{2,1,0:T(4,128)(2,1)S(1)} %prep.1.refs_0_), channel_id=1, source_target_pairs={{0,24},{1,25},{2,26},{3,27},{4,28},{5,29},{6,30},{7,31},{8,16},{9,... | collective-permute-start | bytes 104456 | tf_op jit(solution)/shard_map/ppermute | solution.py:46
  6.8 0.6 %collective-permute-start = (bf16[2,4,2176]{2,1,0:T(4,128)(2,1)S(1)}, bf16[2,4,2176]{2,1,0:T(4,128)(2,1)S(1)}, u32[]{:S(2)}, u32[]{:S(2)}) collective-permute-start(bf16[2,4,2176]{2,1,0:T(4,128)(2,1)S(1)} %prep.1.refs_0_), channel_id=1, source_target_pairs={{0,8},{1,9},{2,10},{3,11},{4,12},{5,13},{6,14},{7,15},{8,0},{9,1},... | collective-permute-start | bytes 104456 | tf_op jit(solution)/shard_map/ppermute | solution.py:46
  7.4 1.3 %collective-permute-done.2.refs_3_ = bf16[2,4,2176]{2,1,0:T(4,128)(2,1)S(1)} collective-permute-done((bf16[2,4,2176]{2,1,0:T(4,128)(2,1)S(1)}, bf16[2,4,2176]{2,1,0:T(4,128)(2,1)S(1)}, u32[]{:S(2)}, u32[]{:S(2)}) %collective-permute-start.2) | collective-permute-done | bytes 34848 | tf_op jit(solution)/shard_map/ppermute | solution.py:46
  8.7 2.9 %collective-permute-done.1.refs_2_ = bf16[2,4,2176]{2,1,0:T(4,128)(2,1)S(1)} collective-permute-done((bf16[2,4,2176]{2,1,0:T(4,128)(2,1)S(1)}, bf16[2,4,2176]{2,1,0:T(4,128)(2,1)S(1)}, u32[]{:S(2)}, u32[]{:S(2)}) %collective-permute-start.1) | collective-permute-done | bytes 34848 | tf_op jit(solution)/shard_map/ppermute | solution.py:46
  11.6 2.5 %collective-permute-start.5 = (bf16[32,2176]{1,0:T(8,128)(2,1)S(1)}, bf16[32,2176]{1,0:T(8,128)(2,1)S(1)}, u32[]{:S(2)}, u32[]{:S(2)}) collective-permute-start(bf16[32,2176]{1,0:T(8,128)(2,1)S(1)} %join.1.block_in.refs_0_), channel_id=1, source_target_pairs={{0,5},{1,4},{2,7},{3,6},{4,1},{5,0},{6,3},{7,2},{8,13},{9,12},{10,... | collective-permute-start | bytes 417800 | tf_op jit(solution)/shard_map/ppermute | solution.py:46
  14.2 0.5 %collective-permute-start.4 = (bf16[32,2176]{1,0:T(8,128)(2,1)S(1)}, bf16[32,2176]{1,0:T(8,128)(2,1)S(1)}, u32[]{:S(2)}, u32[]{:S(2)}) collective-permute-start(bf16[32,2176]{1,0:T(8,128)(2,1)S(1)} %join.1.block_in.refs_0_), channel_id=1, source_target_pairs={{0,4},{1,5},{2,6},{3,7},{4,0},{5,1},{6,2},{7,3},{8,12},{9,13},{10,... | collective-permute-start | bytes 417800 | tf_op jit(solution)/shard_map/ppermute | solution.py:46
  14.7 0.5 %collective-permute-start.3 = (bf16[32,2176]{1,0:T(8,128)(2,1)S(1)}, bf16[32,2176]{1,0:T(8,128)(2,1)S(1)}, u32[]{:S(2)}, u32[]{:S(2)}) collective-permute-start(bf16[32,2176]{1,0:T(8,128)(2,1)S(1)} %join.1.block_in.refs_0_), channel_id=1, source_target_pairs={{0,1},{1,0},{2,3},{3,2},{4,5},{5,4},{6,7},{7,6},{8,9},{9,8},{10,11... | collective-permute-start | bytes 417800 | tf_op jit(solution)/shard_map/ppermute | solution.py:46
  15.2 2.5 %load.1 = (bf16[32,2176]{1,0:T(8,128)(2,1)S(1)}, bf16[2048,768]{1,0:T(8,128)(2,1)S(1)}, bf16[384,2048]{1,0:T(8,128)(2,1)S(1)}) custom-call(bf16[32,2176]{1,0:T(8,128)(2,1)S(1)} %join.1.block_in.refs_0_, bf16[1,2048,384]{2,1,0:T(8,128)(2,1)} %gate_in.1, bf16[1,2048,384]{2,1,0:T(8,128)(2,1)} %up_in.1, bf16[1,384,2048]{2,1,0:T(8,128)(2,1)} %down_in.1), custom_call_target="tpu_custom_call" | custom-call | bytes 9437184 | tf_op jit(solution)/shard_map/load/pallas_call | solution.py:411
  17.7 0.1 collective-permute-start.6
  17.8 1.4 %collective-permute-done.5.refs_3_ = bf16[32,2176]{1,0:T(8,128)(2,1)S(1)} collective-permute-done((bf16[32,2176]{1,0:T(8,128)(2,1)S(1)}, bf16[32,2176]{1,0:T(8,128)(2,1)S(1)}, u32[]{:S(2)}, u32[]{:S(2)}) %collective-permute-start.5) | collective-permute-done | bytes 139296 | tf_op jit(solution)/shard_map/ppermute | solution.py:46
  19.2 0.8 %collective-permute-done.4.refs_2_ = bf16[32,2176]{1,0:T(8,128)(2,1)S(1)} collective-permute-done((bf16[32,2176]{1,0:T(8,128)(2,1)S(1)}, bf16[32,2176]{1,0:T(8,128)(2,1)S(1)}, u32[]{:S(2)}, u32[]{:S(2)}) %collective-permute-start.4) | collective-permute-done | bytes 139296 | tf_op jit(solution)/shard_map/ppermute | solution.py:46
  19.9 0.5 %collective-permute-start.7 = (bf16[32,2176]{1,0:T(8,128)(2,1)S(1)}, bf16[32,2176]{1,0:T(8,128)(2,1)S(1)}, u32[]{:S(2)}, u32[]{:S(2)}) collective-permute-start(bf16[32,2176]{1,0:T(8,128)(2,1)S(1)} %collective-permute-done.3.refs_1_), channel_id=1, source_target_pairs={{0,2},{1,3},{2,0},{3,1},{4,6},{5,7},{6,4},{7,5},{8,10},{9,11},{10,... | collective-permute-start | bytes 417800 | tf_op jit(solution)/shard_map/ppermute | solution.py:46
  20.5 0.8 %collective-permute-done.8.refs_6_ = bf16[32,2176]{1,0:T(8,128)(2,1)S(1)} collective-permute-done((bf16[32,2176]{1,0:T(8,128)(2,1)S(1)}, bf16[32,2176]{1,0:T(8,128)(2,1)S(1)}, u32[]{:S(2)}, u32[]{:S(2)}) %collective-permute-start.8) | collective-permute-done | bytes 139296 | tf_op jit(solution)/shard_map/ppermute | solution.py:46
  21.3 0.2 collective-permute-done.7.refs_5_
  21.5 2.1 %units.1 = (f32[64,2048]{1,0:T(8,128)S(1)}, bf16[64,2176]{1,0:T(8,128)(2,1)S(1)}, f32[2,128]{1,0:T(2,128)S(1)}) custom-call(bf16[32,2176]{1,0:T(8,128)(2,1)S(1)} %join.1.block_in.refs_0_, bf16[32,2176]{1,0:T(8,128)(2,1)S(1)} %collective-permute-done.3.refs_1_, bf16[32,2176]{1,0:T(8,128)(2,1)S(1)} %collective-permute-done.4.refs_2_, ...), custom_call_target="tpu_custom_call" | custom-call | flops 1006632960 | bytes 5767168 | tf_op jit(solution)/shard_map/units/pallas_call | solution.py:433
  23.6 0.4 collective-permute-start.10
  24.0 1.2 %collective-permute-done.10.refs_2_ = bf16[64,2176]{1,0:T(8,128)(2,1)S(1)} collective-permute-done((bf16[64,2176]{1,0:T(8,128)(2,1)S(1)}, bf16[64,2176]{1,0:T(8,128)(2,1)S(1)}, u32[]{:S(2)}, u32[]{:S(2)}) %collective-permute-start.10) | collective-permute-done | bytes 278560 | tf_op jit(solution)/shard_map/ppermute | solution.py:46
  25.2 0.1 add.2
  25.3 1.2 %collective-permute-start.11 = (bf16[16,2176]{1,0:T(8,128)(2,1)S(1)}, bf16[16,2176]{1,0:T(8,128)(2,1)S(1)}, u32[]{:S(2)}, u32[]{:S(2)}) collective-permute-start(bf16[16,2176]{1,0:T(8,128)(2,1)S(1)} %get-tuple-element.34), channel_id=1, source_target_pairs={{0,1},{1,0},{2,3},{3,2},{4,5},{5,4},{6,7},{7,6},{8,9},{9,8},{10,11... | collective-permute-start | bytes 208904 | tf_op jit(solution)/shard_map/ppermute | solution.py:46
  26.5 1.5 %collective-permute-start.12 = (bf16[16,2176]{1,0:T(8,128)(2,1)S(1)}, bf16[16,2176]{1,0:T(8,128)(2,1)S(1)}, u32[]{:S(2)}, u32[]{:S(2)}) collective-permute-start(bf16[16,2176]{1,0:T(8,128)(2,1)S(1)} %get-tuple-element.35), channel_id=1, source_target_pairs={{0,5},{1,4},{2,7},{3,6},{4,1},{5,0},{6,3},{7,2},{8,13},{9,12},{10,... | collective-permute-start | bytes 208904 | tf_op jit(solution)/shard_map/ppermute | solution.py:46
  28.0 0.8 %collective-permute-start.13 = (bf16[16,2176]{1,0:T(8,128)(2,1)S(1)}, bf16[16,2176]{1,0:T(8,128)(2,1)S(1)}, u32[]{:S(2)}, u32[]{:S(2)}) collective-permute-start(bf16[16,2176]{1,0:T(8,128)(2,1)S(1)} %get-tuple-element.36), channel_id=1, source_target_pairs={{0,4},{1,5},{2,6},{3,7},{4,0},{5,1},{6,2},{7,3},{8,12},{9,13},{10,... | collective-permute-start | bytes 208904 | tf_op jit(solution)/shard_map/ppermute | solution.py:46
  28.9 1.4 %collective-permute-done.11.refs_2_ = bf16[16,2176]{1,0:T(8,128)(2,1)S(1)} collective-permute-done((bf16[16,2176]{1,0:T(8,128)(2,1)S(1)}, bf16[16,2176]{1,0:T(8,128)(2,1)S(1)}, u32[]{:S(2)}, u32[]{:S(2)}) %collective-permute-start.11) | collective-permute-done | bytes 69664 | tf_op jit(solution)/shard_map/ppermute | solution.py:46
  30.2 1.7 %collective-permute-done.12.refs_3_ = bf16[16,2176]{1,0:T(8,128)(2,1)S(1)} collective-permute-done((bf16[16,2176]{1,0:T(8,128)(2,1)S(1)}, bf16[16,2176]{1,0:T(8,128)(2,1)S(1)}, u32[]{:S(2)}, u32[]{:S(2)}) %collective-permute-start.12) | collective-permute-done | bytes 69664 | tf_op jit(solution)/shard_map/ppermute | solution.py:46
  32.0 1.2 %collective-permute-done.13.refs_4_ = bf16[16,2176]{1,0:T(8,128)(2,1)S(1)} collective-permute-done((bf16[16,2176]{1,0:T(8,128)(2,1)S(1)}, bf16[16,2176]{1,0:T(8,128)(2,1)S(1)}, u32[]{:S(2)}, u32[]{:S(2)}) %collective-permute-start.13) | collective-permute-done | bytes 69664 | tf_op jit(solution)/shard_map/ppermute | solution.py:46
  33.2 1.9 %collective-permute-start.14 = (bf16[4,2560]{1,0:T(4,128)(2,1)S(1)}, bf16[4,2560]{1,0:T(4,128)(2,1)S(1)}, u32[]{:S(2)}, u32[]{:S(2)}) collective-permute-start(bf16[4,2560]{1,0:T(4,128)(2,1)S(1)} %get-tuple-element.39), channel_id=1, source_target_pairs={{0,24},{1,25},{2,26},{3,27},{4,28},{5,29},{6,30},{7,31},{8,16},{9,... | collective-permute-start | bytes 61448 | tf_op jit(solution)/shard_map/ppermute | solution.py:46
  35.1 0.2 collective-permute-start.15
  35.4 2.3 %collective-permute-start.16 = (bf16[4,2560]{1,0:T(4,128)(2,1)S(1)}, bf16[4,2560]{1,0:T(4,128)(2,1)S(1)}, u32[]{:S(2)}, u32[]{:S(2)}) collective-permute-start(bf16[4,2560]{1,0:T(4,128)(2,1)S(1)} %get-tuple-element.41), channel_id=1, source_target_pairs={{0,8},{1,9},{2,10},{3,11},{4,12},{5,13},{6,14},{7,15},{8,0},{9,1},... | collective-permute-start | bytes 61448 | tf_op jit(solution)/shard_map/ppermute | solution.py:46
  37.7 0.4 tables.1
  38.0 0.8 %collective-permute-done.14.refs_6_ = bf16[4,2560]{1,0:T(4,128)(2,1)S(1)} collective-permute-done((bf16[4,2560]{1,0:T(4,128)(2,1)S(1)}, bf16[4,2560]{1,0:T(4,128)(2,1)S(1)}, u32[]{:S(2)}, u32[]{:S(2)}) %collective-permute-start.14) | collective-permute-done | bytes 20512 | tf_op jit(solution)/shard_map/ppermute | solution.py:46
  38.9 1.0 %collective-permute-done.15.refs_7_ = bf16[4,2560]{1,0:T(4,128)(2,1)S(1)} collective-permute-done((bf16[4,2560]{1,0:T(4,128)(2,1)S(1)}, bf16[4,2560]{1,0:T(4,128)(2,1)S(1)}, u32[]{:S(2)}, u32[]{:S(2)}) %collective-permute-start.15) | collective-permute-done | bytes 20512 | tf_op jit(solution)/shard_map/ppermute | solution.py:46
  39.8 1.1 %final.1 = (bf16[4,2048]{1,0:T(4,128)(2,1)}, f32[16,64]{1,0:T(8,128)}) custom-call(f32[16,128]{1,0:T(8,128)S(1)} %get-tuple-element.30.refs_0_, bf16[128,128]{1,0:T(8,128)(2,1)S(1)} %get-tuple-element.31.refs_1_, bf16[16,128]{1,0:T(8,128)(2,1)S(1)} %get-tuple-element.32.refs_2_, bf16[16,2048]{1,0:T(8,128)(2,1)S(1)} %bitcast.2, ...), custom_call_target="tpu_custom_call" | custom-call | tf_op jit(solution)/shard_map/final/pallas_call | solution.py:500
  (12 shorter events, 0.2 us)
Async XLA Ops:
  1.6 7.0 %collective-permute-start.2 = (bf16[2,4,2176]{2,1,0:T(4,128)(2,1)S(1)}, bf16[2,4,2176]{2,1,0:T(4,128)(2,1)S(1)}, u32[]{:S(2)}, u32[]{:S(2)}) collective-permute-start(bf16[2,4,2176]{2,1,0:T(4,128)(2,1)S(1)} %prep.1.refs_0_), channel_id=1, source_target_pairs={{0,24},{1,25},{2,26},{3,27},{4,28},{5,29},{6,30},{7,31},{8,16},{9,... | collective-permute-start | bytes 104456 | tf_op jit(solution)/shard_map/ppermute | solution.py:46
  6.8 4.8 %collective-permute-start.1 = (bf16[2,4,2176]{2,1,0:T(4,128)(2,1)S(1)}, bf16[2,4,2176]{2,1,0:T(4,128)(2,1)S(1)}, u32[]{:S(2)}, u32[]{:S(2)}) collective-permute-start(bf16[2,4,2176]{2,1,0:T(4,128)(2,1)S(1)} %prep.1.refs_0_), channel_id=1, source_target_pairs={{0,16},{1,17},{2,18},{3,19},{4,20},{5,21},{6,22},{7,23},{8,24},{9,... | collective-permute-start | bytes 104456 | tf_op jit(solution)/shard_map/ppermute | solution.py:46
  6.8 4.8 %collective-permute-start = (bf16[2,4,2176]{2,1,0:T(4,128)(2,1)S(1)}, bf16[2,4,2176]{2,1,0:T(4,128)(2,1)S(1)}, u32[]{:S(2)}, u32[]{:S(2)}) collective-permute-start(bf16[2,4,2176]{2,1,0:T(4,128)(2,1)S(1)} %prep.1.refs_0_), channel_id=1, source_target_pairs={{0,8},{1,9},{2,10},{3,11},{4,12},{5,13},{6,14},{7,15},{8,0},{9,1},... | collective-permute-start | bytes 104456 | tf_op jit(solution)/shard_map/ppermute | solution.py:46
  11.6 7.5 %collective-permute-start.5 = (bf16[32,2176]{1,0:T(8,128)(2,1)S(1)}, bf16[32,2176]{1,0:T(8,128)(2,1)S(1)}, u32[]{:S(2)}, u32[]{:S(2)}) collective-permute-start(bf16[32,2176]{1,0:T(8,128)(2,1)S(1)} %join.1.block_in.refs_0_), channel_id=1, source_target_pairs={{0,5},{1,4},{2,7},{3,6},{4,1},{5,0},{6,3},{7,2},{8,13},{9,12},{10,... | collective-permute-start | bytes 417800 | tf_op jit(solution)/shard_map/ppermute | solution.py:46
  14.2 5.8 %collective-permute-start.4 = (bf16[32,2176]{1,0:T(8,128)(2,1)S(1)}, bf16[32,2176]{1,0:T(8,128)(2,1)S(1)}, u32[]{:S(2)}, u32[]{:S(2)}) collective-permute-start(bf16[32,2176]{1,0:T(8,128)(2,1)S(1)} %join.1.block_in.refs_0_), channel_id=1, source_target_pairs={{0,4},{1,5},{2,6},{3,7},{4,0},{5,1},{6,2},{7,3},{8,12},{9,13},{10,... | collective-permute-start | bytes 417800 | tf_op jit(solution)/shard_map/ppermute | solution.py:46
  14.7 5.3 %collective-permute-start.3 = (bf16[32,2176]{1,0:T(8,128)(2,1)S(1)}, bf16[32,2176]{1,0:T(8,128)(2,1)S(1)}, u32[]{:S(2)}, u32[]{:S(2)}) collective-permute-start(bf16[32,2176]{1,0:T(8,128)(2,1)S(1)} %join.1.block_in.refs_0_), channel_id=1, source_target_pairs={{0,1},{1,0},{2,3},{3,2},{4,5},{5,4},{6,7},{7,6},{8,9},{9,8},{10,11... | collective-permute-start | bytes 417800 | tf_op jit(solution)/shard_map/ppermute | solution.py:46
  17.7 2.8 %collective-permute-start.6 = (bf16[32,2176]{1,0:T(8,128)(2,1)S(1)}, bf16[32,2176]{1,0:T(8,128)(2,1)S(1)}, u32[]{:S(2)}, u32[]{:S(2)}) collective-permute-start(bf16[32,2176]{1,0:T(8,128)(2,1)S(1)} %get-tuple-element.23), channel_id=1, source_target_pairs={{0,2},{1,3},{2,0},{3,1},{4,6},{5,7},{6,4},{7,5},{8,10},{9,11},{10,... | collective-permute-start | bytes 417800 | tf_op jit(solution)/shard_map/ppermute | solution.py:46
  19.2 1.4 %collective-permute-start.9 = (bf16[32,2176]{1,0:T(8,128)(2,1)S(1)}, bf16[32,2176]{1,0:T(8,128)(2,1)S(1)}, u32[]{:S(2)}, u32[]{:S(2)}) collective-permute-start(bf16[32,2176]{1,0:T(8,128)(2,1)S(1)} %collective-permute-done.5.refs_3_), channel_id=1, source_target_pairs={{0,2},{1,3},{2,0},{3,1},{4,6},{5,7},{6,4},{7,5},{8,10},{9,11},{10,... | collective-permute-start | bytes 417800 | tf_op jit(solution)/shard_map/ppermute | solution.py:46
  19.9 1.4 %collective-permute-start.8 = (bf16[32,2176]{1,0:T(8,128)(2,1)S(1)}, bf16[32,2176]{1,0:T(8,128)(2,1)S(1)}, u32[]{:S(2)}, u32[]{:S(2)}) collective-permute-start(bf16[32,2176]{1,0:T(8,128)(2,1)S(1)} %collective-permute-done.4.refs_2_), channel_id=1, source_target_pairs={{0,2},{1,3},{2,0},{3,1},{4,6},{5,7},{6,4},{7,5},{8,10},{9,11},{10,... | collective-permute-start | bytes 417800 | tf_op jit(solution)/shard_map/ppermute | solution.py:46
  19.9 1.6 %collective-permute-start.7 = (bf16[32,2176]{1,0:T(8,128)(2,1)S(1)}, bf16[32,2176]{1,0:T(8,128)(2,1)S(1)}, u32[]{:S(2)}, u32[]{:S(2)}) collective-permute-start(bf16[32,2176]{1,0:T(8,128)(2,1)S(1)} %collective-permute-done.3.refs_1_), channel_id=1, source_target_pairs={{0,2},{1,3},{2,0},{3,1},{4,6},{5,7},{6,4},{7,5},{8,10},{9,11},{10,... | collective-permute-start | bytes 417800 | tf_op jit(solution)/shard_map/ppermute | solution.py:46
  23.6 1.6 %collective-permute-start.10 = (bf16[64,2176]{1,0:T(8,128)(2,1)S(1)}, bf16[64,2176]{1,0:T(8,128)(2,1)S(1)}, u32[]{:S(2)}, u32[]{:S(2)}) collective-permute-start(bf16[64,2176]{1,0:T(8,128)(2,1)S(1)} %get-tuple-element.28), channel_id=1, source_target_pairs={{0,2},{1,3},{2,0},{3,1},{4,6},{5,7},{6,4},{7,5},{8,10},{9,11},{10,... | collective-permute-start | bytes 835592 | tf_op jit(solution)/shard_map/ppermute | solution.py:46
  25.3 4.9 %collective-permute-start.11 = (bf16[16,2176]{1,0:T(8,128)(2,1)S(1)}, bf16[16,2176]{1,0:T(8,128)(2,1)S(1)}, u32[]{:S(2)}, u32[]{:S(2)}) collective-permute-start(bf16[16,2176]{1,0:T(8,128)(2,1)S(1)} %get-tuple-element.34), channel_id=1, source_target_pairs={{0,1},{1,0},{2,3},{3,2},{4,5},{5,4},{6,7},{7,6},{8,9},{9,8},{10,11... | collective-permute-start | bytes 208904 | tf_op jit(solution)/shard_map/ppermute | solution.py:46
  26.5 5.5 %collective-permute-start.12 = (bf16[16,2176]{1,0:T(8,128)(2,1)S(1)}, bf16[16,2176]{1,0:T(8,128)(2,1)S(1)}, u32[]{:S(2)}, u32[]{:S(2)}) collective-permute-start(bf16[16,2176]{1,0:T(8,128)(2,1)S(1)} %get-tuple-element.35), channel_id=1, source_target_pairs={{0,5},{1,4},{2,7},{3,6},{4,1},{5,0},{6,3},{7,2},{8,13},{9,12},{10,... | collective-permute-start | bytes 208904 | tf_op jit(solution)/shard_map/ppermute | solution.py:46
  28.0 5.1 %collective-permute-start.13 = (bf16[16,2176]{1,0:T(8,128)(2,1)S(1)}, bf16[16,2176]{1,0:T(8,128)(2,1)S(1)}, u32[]{:S(2)}, u32[]{:S(2)}) collective-permute-start(bf16[16,2176]{1,0:T(8,128)(2,1)S(1)} %get-tuple-element.36), channel_id=1, source_target_pairs={{0,4},{1,5},{2,6},{3,7},{4,0},{5,1},{6,2},{7,3},{8,12},{9,13},{10,... | collective-permute-start | bytes 208904 | tf_op jit(solution)/shard_map/ppermute | solution.py:46
  33.2 5.6 %collective-permute-start.14 = (bf16[4,2560]{1,0:T(4,128)(2,1)S(1)}, bf16[4,2560]{1,0:T(4,128)(2,1)S(1)}, u32[]{:S(2)}, u32[]{:S(2)}) collective-permute-start(bf16[4,2560]{1,0:T(4,128)(2,1)S(1)} %get-tuple-element.39), channel_id=1, source_target_pairs={{0,24},{1,25},{2,26},{3,27},{4,28},{5,29},{6,30},{7,31},{8,16},{9,... | collective-permute-start | bytes 61448 | tf_op jit(solution)/shard_map/ppermute | solution.py:46
  35.1 4.7 %collective-permute-start.15 = (bf16[4,2560]{1,0:T(4,128)(2,1)S(1)}, bf16[4,2560]{1,0:T(4,128)(2,1)S(1)}, u32[]{:S(2)}, u32[]{:S(2)}) collective-permute-start(bf16[4,2560]{1,0:T(4,128)(2,1)S(1)} %get-tuple-element.40), channel_id=1, source_target_pairs={{0,16},{1,17},{2,18},{3,19},{4,20},{5,21},{6,22},{7,23},{8,24},{9,... | collective-permute-start | bytes 61448 | tf_op jit(solution)/shard_map/ppermute | solution.py:46
  35.4 4.5 %copy-start = (bf16[2048,16]{0,1:T(8,128)(2,1)S(1)}, bf16[2048,16]{0,1:T(8,128)(2,1)}, u32[]{:S(2)}) copy-start(bf16[2048,16]{0,1:T(8,128)(2,1)} %param.12) | copy-start | bytes 196612
  35.4 4.4 %collective-permute-start.16 = (bf16[4,2560]{1,0:T(4,128)(2,1)S(1)}, bf16[4,2560]{1,0:T(4,128)(2,1)S(1)}, u32[]{:S(2)}, u32[]{:S(2)}) collective-permute-start(bf16[4,2560]{1,0:T(4,128)(2,1)S(1)} %get-tuple-element.41), channel_id=1, source_target_pairs={{0,8},{1,9},{2,10},{3,11},{4,12},{5,13},{6,14},{7,15},{8,0},{9,1},... | collective-permute-start | bytes 61448 | tf_op jit(solution)/shard_map/ppermute | solution.py:46
